TPU v7x, 1024 devices: a whole 4x4x32 slice. The times are simulated.
1024 devices in a mesh: dp: 4 (over x), expert: 16 (over y, z_hi), tensor: 16 (over z_lo, core).
Axes of the slice: x: 4, y: 4, z: 32 (z_hi: 4, z_lo: 8; z = z_hi * 8 + z_lo), core: 2. Of those that a mesh axis runs over, the one named last changes fastest.
Arguments:
- grad_out: bfloat16 [2048, 6144], P(('dp', 'expert', 'tensor')), may hold values from -6 to 6
- route_ids: int32 [2048, 4], P(('dp', 'expert', 'tensor')), may hold values from 0 to 15, all different within a row; in each aligned block of 32 rows (0 to 31, 32 to 63, ...) at most 10 rows name the same one
- route_probs: bfloat16 [2048, 4], P(('dp', 'expert', 'tensor')), may hold values from 0.099609375 to 1
- gate_up: bfloat16 [4, 16, 16, 10, 2, 5376], P('dp', 'expert', None, None, None, 'tensor'), may hold values from -5 to 5
- w_down: bfloat16 [16, 5376, 6144], P('expert', 'tensor'), may hold values from -0.078125 to 0.078125
Outputs:
- grad_pre: bfloat16 [4, 16, 16, 10, 2, 5376], P('dp', 'expert', None, None, None, 'tensor')
- grad_w_down: bfloat16 [16, 5376, 6144], P('expert', 'tensor', 'dp')
Inputs may be any that keep to these rules, and one draw needn't show every extreme that they name: `route_ids`: in each aligned block of 32 tokens no expert is named by more than 10 of them; a token names distinct experts.
All inputs are finite; a program needn't handle non-finite values.
Results may differ from a plain program's by a relative error of at most 0.013.
Values may be sent and summed in bfloat16 or wider, within the bound.
A program may use at most 32 MiB of HBM per device.

v0:
```python
import jax
import jax.numpy as jnp
from jax import lax
from jax.sharding import PartitionSpec as P


def per_device(grad_out, route_ids, route_probs, gate_up, w_down):
    cot, ids, probs = (
        lax.all_gather(grad_out, "tensor", axis=0, tiled=True),
        lax.all_gather(route_ids, "tensor", axis=0, tiled=True),
        lax.all_gather(route_probs, "tensor", axis=0, tiled=True),
    )
    experts_all = lax.axis_size("expert")
    width = ids.shape[0] * ids.shape[1]
    model_width = cot.shape[1]
    slots = gate_up.shape[3]
    hidden_width = gate_up.shape[5]
    flat_ids = ids.reshape(width)
    rows = (
        (probs.astype(jnp.float32)[:, :, None] * cot.astype(jnp.float32)[:, None, :])
        .astype(jnp.bfloat16)
        .reshape(width, model_width)
    )
    onehot = (flat_ids[:, None] == jnp.arange(experts_all, dtype=jnp.int32)[None, :]).astype(
        jnp.int32
    )
    place = jnp.sum((jnp.cumsum(onehot, axis=0) - 1) * onehot, axis=1)
    slot = flat_ids * slots + place
    select = (slot[None, :] == jnp.arange(experts_all * slots, dtype=jnp.int32)[:, None]).astype(
        jnp.bfloat16
    )
    outgoing = jnp.dot(select, rows, preferred_element_type=jnp.float32).astype(jnp.bfloat16)
    outgoing = outgoing.reshape(experts_all, slots, model_width)
    received = lax.all_to_all(outgoing, "expert", split_axis=0, concat_axis=0, tiled=True)
    count = received.shape[0] * slots
    flat = received.reshape(count, model_width)
    weight = w_down[0]
    grad_hidden = lax.dot_general(
        flat, weight, (((1,), (1,)), ((), ())), preferred_element_type=jnp.float32
    )
    saved = gate_up[0, 0].astype(jnp.float32).reshape(count, 2, hidden_width)
    gate = saved[:, 0]
    upper = saved[:, 1]
    sig = jax.nn.sigmoid(gate)
    d_gate = grad_hidden * upper * sig * (1.0 + gate * (1.0 - sig))
    d_upper = grad_hidden * gate * sig
    grad_pre = jnp.stack([d_gate, d_upper], axis=1).astype(jnp.bfloat16).reshape(gate_up.shape)
    hidden = (gate * sig * upper).astype(jnp.bfloat16)
    owned = lax.psum_scatter(
        lax.dot_general(
            flat, hidden, (((0,), (0,)), ((), ())), preferred_element_type=jnp.float32
        ).astype(jnp.bfloat16),
        "dp",
        scatter_dimension=0,
        tiled=True,
    ).astype(jnp.float32)
    grad_w = owned.T.astype(jnp.bfloat16)
    return (grad_pre, grad_w[None])


def solution(mesh):
    return jax.shard_map(
        per_device,
        mesh=mesh,
        in_specs=(
            P(("dp", "expert", "tensor"), None),
            P(("dp", "expert", "tensor"), None),
            P(("dp", "expert", "tensor"), None),
            P("dp", "expert", None, None, None, "tensor"),
            P("expert", "tensor", None),
        ),
        out_specs=(P("dp", "expert", None, None, None, "tensor"), P("expert", "tensor", "dp")),
        check_vma=False,
    )
```

profile of v0, /device:TPU:1, one launch (start us, length us, event | category | flops | bytes accessed | tf_op | source)
XLA Modules:
  0.0 498.7 jit_solution(16243660714527633429)
XLA Ops:
  7.2 39.0 %all-gather.1 = bf16[16,2,4]{2,1,0:T(2,128)(2,1)S(1)} all-gather(bf16[1,2,4]{2,1,0:T(2,128)(2,1)} %bitcast.51), channel_id=1, replica_groups=mesh['dp'=4,'expert'=16,'tensor'=16] {'tensor'}, dimensions={0}, use_global_device_ids=true | all-gather | bytes 272 | tf_op jit(solution)/shard_map/all_gather | solution.py:11
  46.2 0.1 reshape.71
  46.3 27.1 %all-gather = s32[16,2,4]{2,1,0:T(2,128)S(1)} all-gather(s32[1,2,4]{2,1,0:T(2,128)} %bitcast.50), channel_id=1, replica_groups=mesh['dp'=4,'expert'=16,'tensor'=16] {'tensor'}, dimensions={0}, use_global_device_ids=true | all-gather | bytes 544 | tf_op jit(solution)/shard_map/all_gather | solution.py:10
  73.4 0.1 reshape.68
  73.5 0.1 fusion.13
  73.6 0.2 reduce_window_sum.11
  73.8 0.2 select_reduce_fusion
  74.0 27.1 %all-gather.2 = bf16[16,2,6144]{2,1,0:T(2,128)(2,1)S(1)} all-gather(bf16[1,2,6144]{2,1,0:T(2,128)(2,1)} %bitcast.49), channel_id=1, replica_groups=mesh['dp'=4,'expert'=16,'tensor'=16] {'tensor'}, dimensions={0}, use_global_device_ids=true | all-gather | bytes 417792 | tf_op jit(solution)/shard_map/all_gather | solution.py:9
  101.1 0.1 reshape.79
  101.2 2.5 mul.65
  103.7 3.1 mul.66
  106.9 2.0 convolution_convert_fusion.1
  108.9 4.2 reshape.69
  113.1 0.0 copy-start
  113.1 21.7 %all-to-all-start = ((bf16[16,10,6144]{2,1,0:T(8,128)(2,1)}), bf16[16,10,6144]{2,1,0:T(8,128)(2,1)}, u32[]{:S(2)}, u32[]{:S(2)}) async-start(bf16[16,10,6144]{2,1,0:T(8,128)(2,1)} %reshape.69), calls=%async_computation | async-start | bytes 6291456 | tf_op jit(solution)/shard_map/all_to_all | solution.py:34
  134.8 0.0 reduce-scatter.2.cloned.1.call-start
  134.9 0.0 copy-done
  134.9 0.2 bitcast_convert_fusion
  135.1 0.4 fusion.16
  135.5 265.3 %all-to-all-done = bf16[16,10,6144]{2,1,0:T(8,128)(2,1)} async-done(((bf16[16,10,6144]{2,1,0:T(8,128)(2,1)}), bf16[16,10,6144]{2,1,0:T(8,128)(2,1)}, u32[]{:S(2)}, u32[]{:S(2)}) %all-to-all-start) | async-done | bytes 1966112 | tf_op jit(solution)/shard_map/all_to_all | solution.py:34
  400.8 3.0 reshape.70
  403.7 3.2 convolution_convert_fusion
  406.9 0.0 reduce-scatter.2.cloned.1.call-update
  407.0 3.8 fusion.8
  410.8 0.1 stack.9
  410.8 0.1 stack.10
  410.9 0.1 pad_maximum_fusion
  411.0 0.9 copy.15
  412.0 79.9 %reduce-scatter.2.cloned.1.call-done = bf16[1536,336]{0,1:T(8,128)(2,1)} async-done(((bf16[6144,336]{0,1:T(8,128)(2,1)}), bf16[1536,336]{0,1:T(8,128)(2,1)}) %reduce-scatter.2.cloned.1.call-update) | async-done | bytes 1032208 | tf_op jit(solution)/shard_map/reduce_scatter | solution.py:49
  (1 shorter events, 0.0 us)
Async XLA Ops:
  113.1 21.7 %copy-start = (bf16[1,1,16,10,2,336]{5,4,3,2,1,0:T(2,128)(2,1)S(1)}, bf16[1,1,16,10,2,336]{5,4,3,2,1,0:T(2,128)(2,1)}, u32[]{:S(2)}) copy-start(bf16[1,1,16,10,2,336]{5,4,3,2,1,0:T(2,128)(2,1)} %param.8) | copy-start | bytes 645124
  113.1 287.6 %all-to-all-start = ((bf16[16,10,6144]{2,1,0:T(8,128)(2,1)}), bf16[16,10,6144]{2,1,0:T(8,128)(2,1)}, u32[]{:S(2)}, u32[]{:S(2)}) async-start(bf16[16,10,6144]{2,1,0:T(8,128)(2,1)} %reshape.69), calls=%async_computation | async-start | bytes 6291456 | tf_op jit(solution)/shard_map/all_to_all | solution.py:34
  134.8 357.0 %reduce-scatter.2.cloned.1.call-start = ((), (), s32[]{:S(2)}) async-start(), calls=%async_computation.2 | async-start | bytes 5160960 | tf_op jit(solution)/shard_map/reduce_scatter | solution.py:49
Sparse Core Ops, SparseCore 0:
  407.1 84.7 reduce-scatter.1
where the time goes:
time: 499 us
  waiting for transfers between devices  345 us (69%)
  blocking collectives  93.2 us (19%)
  starting transfers between devices  21.7 us (4%)
  local copies, waits for them, and re-layouts  14.6 us (3%)
  between operations  14.1 us (3%)
  matrix products  9.08 us (2%)
    all_to_all x1, waiting for transfers between devices, per_device(): lax.all_to_all(outgoing, 'expert', split_axis=0, concat_axis=0, tiled=True)  265 us
    reduce_scatter x1, waiting for transfers between devices, per_device(): lax.psum_scatter(lax.dot_general(flat, hidden, (((0,), (0,)), ((), ())),...  79.9 us
    all_gather x1, blocking collectives, per_device(): lax.all_gather(route_probs, 'tensor', axis=0, tiled=True)  39 us
    all_gather x1, blocking collectives, per_device(): lax.all_gather(grad_out, 'tensor', axis=0, tiled=True)  27.1 us
    all_gather x1, blocking collectives, per_device(): lax.all_gather(route_ids, 'tensor', axis=0, tiled=True)  27.1 us
    all_to_all x1, starting transfers between devices, per_device(): lax.all_to_all(outgoing, 'expert', split_axis=0, concat_axis=0, tiled=True)  21.7 us
  transfers between devices with their start and end apart: 2, of which 2 were waited for; matrix products, arithmetic and copies ran while one was open for 1% of the time, Pallas kernels for 0%

commit v1 on v0

v1 whole, which is shorter than its diff:
```python
import jax
import jax.numpy as jnp
from jax import lax
from jax.experimental import pallas as pl
from jax.experimental.pallas import tpu as pltpu
from jax.sharding import PartitionSpec as P

F32 = jnp.float32
BF16 = jnp.bfloat16
HALF = 768
META = 128
WIDE = HALF + META
SUB = 40
PAD = 48
CHUNK = 160
NT = (((1,), (1,)), ((), ()))


def kernel(ext, gate, up, w_hbm, dgate, dup, gw, stage, tok, ypack, relay, rows, wv, before,
           hid, hid_t, coef_g, coef_u, rs_out, rs_in, w_sem, x_sem, h_sem, a_sem, cw_sem, ccw_sem,
           yr_sem, yd_sem, yf_sem, d_sem, r_sem):
    x, e, t = lax.axis_index("dp"), lax.axis_index("expert"), lax.axis_index("tensor")
    y, zhi = e // 4, e % 4
    zlo, c = t // 2, t % 2
    z = zhi * 8 + zlo
    width = gate.shape[2]

    def at(x_to, y_to, z_to, c_to):
        return (x_to, y_to * 4 + z_to // 8, (z_to % 8) * 2 + c_to)

    def send(src, dst, sems, index, to):
        copy = pltpu.make_async_remote_copy(
            src_ref=src, dst_ref=dst, send_sem=sems.at[(0,) + index], recv_sem=sems.at[(1,) + index],
            device_id=to, device_id_type=pl.DeviceIdType.MESH)
        copy.start()
        return copy

    load_w = pltpu.make_async_copy(
        w_hbm.at[0, :, pl.ds(pl.multiple_of(x * (2 * HALF), 128), 2 * HALF)], wv, w_sem)
    load_w.start()

    next_y, last_y, far_y = (y + 1) % 4, (y + 3) % 4, (y + 2) % 4
    next_z, last_z = (z + 1) % 32, (z + 31) % 32
    sibling = at(x, y, z, 1 - c)
    partners = [at((x + dx) % 4, y, z, (c + dc) % 2) for dx in range(4) for dc in range(2) if dx or dc]
    partners += [at(x, y, (z + 8 * dz) % 32, c) for dz in (1, 2, 3)]
    partners += [at(x, y, next_z, c), at(x, y, last_z, c), at(x, next_y, z, c), at(x, last_y, z, c)]
    barrier = pltpu.get_barrier_semaphore()
    for device in partners:
        pl.semaphore_signal(barrier, inc=1, device_id=device, device_id_type=pl.DeviceIdType.MESH)
    pl.semaphore_wait(barrier, len(partners))

    x_copies = []
    for dx in range(4):
        for dc in range(2):
            if dx or dc:
                xd, cd = (x + dx) % 4, (c + dc) % 2
                x_copies.append(send(ext.at[xd * 2 + cd], stage.at[x * 2 + c], x_sem, (dx * 2 + dc,),
                                     at(xd, y, z, cd)))
    stage[x * 2 + c] = ext[x * 2 + c]

    for part in range(4):
        g, u = gate[part].astype(F32), up[part].astype(F32)
        s = jax.nn.sigmoid(g)
        coef_g[part] = u * s * (1.0 + g * (1.0 - s))
        coef_u[part] = g * s
        hid[x, part, 0:SUB] = (g * s * u).astype(BF16)
        hid[x, part, SUB:PAD] = jnp.zeros((PAD - SUB, width), BF16)
    h_copies = [send(hid.at[x], hid.at[x], h_sem, (dx,), at((x + dx) % 4, y, z, c)) for dx in (1, 2, 3)]

    for copy in x_copies:
        copy.wait_recv()
    tok[zlo, zhi] = stage[...].reshape(16, WIDE)
    a_copies = [send(tok.at[zlo, zhi], tok.at[zlo, zhi], a_sem, (dz,), at(x, y, (z + 8 * dz) % 32, c))
                for dz in (1, 2, 3)]

    from_row = lax.broadcasted_iota(jnp.int32, (512, 512), 0)
    to_row = lax.broadcasted_iota(jnp.int32, (512, 512), 1)
    same = ((from_row >> 2) & 15) == ((to_row >> 2) & 15)
    before[...] = jnp.where(same & (from_row < to_row), 1.0, 0.0).astype(BF16)

    for copy in a_copies:
        copy.wait_recv()

    b_copies = []
    cw, ccw = None, None
    for step in range(4):
        b_next, b_last = (zlo + 8 - step) % 8, (zlo + step) % 8
        if step < 3:
            src_next, src_last = tok.at[b_next], tok.at[b_last]
        else:
            src_next, src_last = tok.at[b_next, pl.ds(0, 2)], tok.at[b_last, pl.ds(2, 2)]
        if cw is not None:
            cw.wait_recv()
        cw = send(src_next, src_next, cw_sem, (step,), at(x, y, next_z, c))
        if ccw is not None:
            ccw.wait_recv()
        ccw = send(src_last, src_last, ccw_sem, (step,), at(x, y, last_z, c))
        b_copies += [cw, ccw]
    cw.wait_recv()
    ccw.wait_recv()

    meta = tok[:, :, :, HALF:WIDE].reshape(512, META)
    pick = (lax.broadcasted_iota(jnp.int32, (8, META), 0) ==
            lax.broadcasted_iota(jnp.int32, (8, META), 1)).astype(F32).astype(BF16)
    meta_t = lax.dot_general(pick, meta, NT, preferred_element_type=F32)
    step_y = lax.broadcasted_iota(jnp.int32, (8, 512), 0)
    expert = (((step_y + y) & 3) * 4 + zhi).astype(F32)
    named = jnp.zeros((8, 512), F32)
    prob = jnp.zeros((8, 512), F32)
    for k in range(4):
        hit = meta_t[k:k + 1, :] == expert
        named = named + jnp.where(hit, 1.0, 0.0)
        prob = prob + jnp.where(hit, meta_t[4 + k:5 + k, :], 0.0)
    place = jnp.dot(named.astype(BF16), before[...], preferred_element_type=F32)
    token = lax.broadcasted_iota(jnp.int32, (8, 512), 1)
    base = (((token >> 2) & 3) * SUB + ((token >> 4) & 3) * 10).astype(F32)
    slot = jnp.where(named > 0.5, base + place, -1.0)
    slots = lax.broadcasted_iota(jnp.int32, (CHUNK, 512), 0).astype(F32)

    def packed(d):
        select = jnp.where(slots == slot[d:d + 1, :], prob[d:d + 1, :], 0.0).astype(BF16)
        data = tok[:, :, :, 0:HALF].reshape(512, HALF)
        return jnp.dot(select, data, preferred_element_type=F32).astype(BF16)

    first, second = pl.ds(0, CHUNK // 2), pl.ds(CHUNK // 2, CHUNK // 2)
    to_next, to_last = at(x, next_y, z, c), at(x, last_y, z, c)
    ypack[2] = packed(2)
    yr_next = send(ypack.at[2, first], relay.at[0], yr_sem, (0,), to_next)
    yr_last = send(ypack.at[2, second], relay.at[1], yr_sem, (1,), to_last)
    ypack[0] = packed(1)
    yd_next = send(ypack.at[0], rows.at[c, y], yd_sem, (0,), to_next)
    ypack[1] = packed(3)
    yd_last = send(ypack.at[1], rows.at[c, y], yd_sem, (1,), to_last)
    rows[c, y] = packed(0)
    d_copies = [send(rows.at[c, y], rows.at[c, y], d_sem, (0,), sibling)]

    for copy in h_copies:
        copy.wait_recv()
    load_w.wait()
    for part in range(4):
        chunk = jnp.concatenate([hid[r, part].astype(F32)[0:SUB] for r in range(4)], axis=0)
        hid_t[part * CHUNK:(part + 1) * CHUNK] = chunk.astype(BF16)

    yr_next.wait_recv()
    yf_next = send(relay.at[0], rows.at[c, last_y, first], yf_sem, (0,), to_next)
    yr_last.wait_recv()
    yf_last = send(relay.at[1], rows.at[c, next_y, second], yf_sem, (1,), to_last)

    r_copies = []

    def partial(i, part):
        d_copies[i].wait_recv()
        gh = lax.dot_general(rows[0, part], wv[:, 0:HALF], NT, preferred_element_type=F32)
        gh = gh + lax.dot_general(rows[1, part], wv[:, HALF:2 * HALF], NT, preferred_element_type=F32)
        for r in range(4):
            rs_out[part, r, 0:SUB] = gh[r * SUB:(r + 1) * SUB].astype(BF16)
            rs_out[part, r, SUB:PAD] = jnp.zeros((PAD - SUB, width), BF16)
        r_copies.append([send(rs_out.at[part, (x + dx) % 4], rs_in.at[x, part], r_sem, (i, dx),
                              at((x + dx) % 4, y, z, c)) for dx in (1, 2, 3)])

    partial(0, y)
    yd_next.wait_recv()
    d_copies.append(send(rows.at[c, last_y], rows.at[c, last_y], d_sem, (1,), sibling))
    yd_last.wait_recv()
    d_copies.append(send(rows.at[c, next_y], rows.at[c, next_y], d_sem, (2,), sibling))
    partial(1, last_y)
    partial(2, next_y)
    yf_next.wait_recv()
    yf_last.wait_recv()
    d_copies.append(send(rows.at[c, far_y], rows.at[c, far_y], d_sem, (3,), sibling))
    partial(3, far_y)

    for core in range(2):
        gw[:, core * HALF:(core + 1) * HALF] = lax.dot_general(
            hid_t[...], rows[core].reshape(4 * CHUNK, HALF), (((0,), (0,)), ((), ())),
            preferred_element_type=F32).astype(BF16)

    for i, part in enumerate((y, last_y, next_y, far_y)):
        for copy in r_copies[i]:
            copy.wait_recv()
        gh = rs_out[part, x].astype(F32)[0:SUB]
        for dx in (1, 2, 3):
            gh = gh + rs_in[(x + dx) % 4, part].astype(F32)[0:SUB]
        dgate[part] = (gh * coef_g[part]).astype(BF16)
        dup[part] = (gh * coef_u[part]).astype(BF16)

    sent = x_copies + h_copies + a_copies + b_copies + d_copies
    sent += [yr_next, yr_last, yd_next, yd_last, yf_next, yf_last]
    for group in r_copies:
        sent += group
    for copy in sent:
        copy.wait_send()


def per_device(grad_out, route_ids, route_probs, gate_up, w_down):
    width = gate_up.shape[5]
    meta = jnp.concatenate([route_ids.astype(BF16), route_probs, jnp.zeros((2, META - 8), BF16)], axis=1)
    cot = jnp.moveaxis(grad_out.reshape(2, 8, HALF), 1, 0)
    ext = jnp.concatenate([cot, jnp.broadcast_to(meta[None], (8, 2, META))], axis=2)
    saved = gate_up.reshape(4, SUB, 2, width)
    vmem = pl.BlockSpec(memory_space=pltpu.VMEM)
    dma = pltpu.SemaphoreType.DMA
    dgate, dup, gw = pl.pallas_call(
        kernel,
        out_shape=(
            jax.ShapeDtypeStruct((4, SUB, width), BF16),
            jax.ShapeDtypeStruct((4, SUB, width), BF16),
            jax.ShapeDtypeStruct((width, 2 * HALF), BF16),
        ),
        in_specs=[vmem, vmem, vmem, pl.BlockSpec(memory_space=pl.ANY)],
        out_specs=(vmem, vmem, vmem),
        scratch_shapes=[
            pltpu.VMEM((8, 2, WIDE), BF16),
            pltpu.VMEM((8, 4, 16, WIDE), BF16),
            pltpu.VMEM((3, CHUNK, HALF), BF16),
            pltpu.VMEM((2, CHUNK // 2, HALF), BF16),
            pltpu.VMEM((2, 4, CHUNK, HALF), BF16),
            pltpu.VMEM((width, 2 * HALF), BF16),
            pltpu.VMEM((512, 512), BF16),
            pltpu.VMEM((4, 4, PAD, width), BF16),
            pltpu.VMEM((4 * CHUNK, width), BF16),
            pltpu.VMEM((4, SUB, width), F32),
            pltpu.VMEM((4, SUB, width), F32),
            pltpu.VMEM((4, 4, PAD, width), BF16),
            pltpu.VMEM((4, 4, PAD, width), BF16),
            dma(()),
            dma((2, 8)),
            dma((2, 4)),
            dma((2, 4)),
            dma((2, 4)),
            dma((2, 4)),
            dma((2, 2)),
            dma((2, 2)),
            dma((2, 2)),
            dma((2, 4)),
            dma((2, 4, 4)),
        ],
        compiler_params=pltpu.CompilerParams(
            collective_id=0, has_side_effects=True, vmem_limit_bytes=48 * 1024 * 1024
        ),
    )(ext, saved[:, :, 0], saved[:, :, 1], w_down)
    grad_pre = jnp.stack([dgate, dup], axis=2).reshape(gate_up.shape)
    return grad_pre, gw[None]


def solution(mesh):
    return jax.shard_map(
        per_device,
        mesh=mesh,
        in_specs=(
            P(("dp", "expert", "tensor"), None),
            P(("dp", "expert", "tensor"), None),
            P(("dp", "expert", "tensor"), None),
            P("dp", "expert", None, None, None, "tensor"),
            P("expert", "tensor", None),
        ),
        out_specs=(P("dp", "expert", None, None, None, "tensor"), P("expert", "tensor", "dp")),
        check_vma=False,
    )
```

time: 499 us -> 95.1 us (0.19)
  waiting for transfers between devices: 345 us -> 0 us
  blocking collectives: 93.2 us -> 0 us
  Pallas kernels: 0 us -> 86.1 us
  starting transfers between devices: 21.7 us -> 0 us
  between operations: 14.1 us -> 0.68 us
  matrix products: 9.08 us -> 0 us
  local copies, waits for them, and re-layouts: 14.6 us -> 5.8 us
    all_to_all x1 -> x0, waiting for transfers between devices: 265 us -> none  [per_device(): lax.all_to_all(outgoing, 'expert', split_axis=0, concat_axis=0, tiled=True)]
    all_gather x3 -> x0, blocking collectives: 93.2 us -> none  [the longest x1 39 us: per_device(): lax.all_gather(route_probs, 'tensor', axis=0, tiled=True)]
    pallas_call x0 -> x1, Pallas kernels: none -> 86.1 us  [per_device(): pl.pallas_call(kernel, out_shape=(jax.ShapeDtypeStruct((4, SUB, width), B...]
    reduce_scatter x1 -> x0, waiting for transfers between devices: 79.9 us -> none  [per_device(): lax.psum_scatter(lax.dot_general(flat, hidden, (((0,), (0,)), ((), ())),...]
    all_to_all x1 -> x0, starting transfers between devices: 21.7 us -> none  [per_device(): lax.all_to_all(outgoing, 'expert', split_axis=0, concat_axis=0, tiled=True)]
    dot_general x3 -> x0, matrix products: 9.08 us -> none  [the longest x1 3.82 us: per_device(): lax.dot_general(flat, weight, (((1,), (1,)), ((), ())), preferred_element...]
    reshape x3 -> x0, local copies, waits for them, and re-layouts: 7.3 us -> none  [the longest x1 4.23 us: per_device(): outgoing = outgoing.reshape(experts_all, slots, model_width)]
    mul x3 -> x0, local copies, waits for them, and re-layouts: 5.75 us -> none  [per_device(): probs.astype(jnp.float32)[:, :, None] * cot.astype(jnp.float32)[:, None, :]]
  transfers between devices with their start and end apart: 2 -> 0, of which waited for: 2 -> 0; matrix products, arithmetic and copies ran while one was open for 1% -> 0% of each run, Pallas kernels for 0% -> 0%
where the time goes in v1:
time: 95.1 us; the launch traced here: 94.8 us
  Pallas kernels  86.1 us (91%)
  local copies, waits for them, and re-layouts  5.8 us (6%)
  other arithmetic  2.27 us (2%)
    pallas_call x1, Pallas kernels, per_device(): pl.pallas_call(kernel, out_shape=(jax.ShapeDtypeStruct((4, SUB, width), B...  86.1 us
    unnamed x4, local copies, waits for them, and re-layouts  4.07 us

profile of v1, /device:TPU:1, one launch (start us, length us, event | category | flops | bytes accessed | tf_op | source)
XLA Modules:
  0.0 94.8 jit_solution(17617396733729894884)
XLA Ops:
  0.6 0.7 convert_element_type.3
  1.3 0.1 pad.6.clone
  1.4 0.7 maximum_maximum_fusion
  2.1 0.8 pad_maximum_fusion.1.ext
  2.9 1.5 %fusion = (bf16[4,40,1,336]{3,2,1,0:T(2,128)(2,1)S(1)}, bf16[4,40,1,336]{3,2,1,0:T(2,128)(2,1)S(1)}) fusion(bf16[4,40,2,336]{3,2,1,0:T(2,128)(2,1)} %bitcast.10), kind=kLoop, calls=%fused_computation.5 | loop fusion | bytes 430080 | tf_op jit(solution)/shard_map/slice | solution.py:242
  4.4 0.0 copy-start
  4.4 2.2 %copy-done = bf16[1,336,6144]{2,1,0:T(8,128)(2,1)S(1)} copy-done((bf16[1,336,6144]{2,1,0:T(8,128)(2,1)S(1)}, bf16[1,336,6144]{2,1,0:T(8,128)(2,1)}, u32[]{:S(2)}) %copy-start) | copy-done | bytes 4128792
  6.6 86.1 %shard_map.68 = (bf16[4,40,336]{2,1,0:T(8,128)(2,1)S(1)}, bf16[4,40,336]{2,1,0:T(8,128)(2,1)S(1)}, bf16[336,1536]{1,0:T(8,128)(2,1)S(1)}) custom-call(bf16[8,2,896]{2,1,0:T(2,128)(2,1)S(1)} %pad_maximum_fusion.1.ext, bf16[4,40,336]{2,1,0:T(8,128)(2,1)S(1)} %get-tuple-element.13.gate, bf16[4,40,336]{2,1,0:T(8,128)(2,1)S(1)} %get-tuple-element.12.up, ...), custom_call_target="tpu_custom_call" | custom-call | tf_op jit(solution)/shard_map/pallas_call | solution.py:204
  92.7 0.1 stack.9
  92.8 0.1 stack.10
  92.8 0.1 pad_maximum_fusion
  92.9 0.9 copy.12
  93.9 1.0 %copy.18 = bf16[1,336,1536]{2,1,0:T(8,128)(2,1)} copy(bf16[1,336,1536]{2,1,0:T(8,128)(2,1)S(1)} %bitcast.9) | data formatting | bytes 2064384
  (3 shorter events, 0.0 us)
Async XLA Ops:
  4.4 2.2 %copy-start = (bf16[1,336,6144]{2,1,0:T(8,128)(2,1)S(1)}, bf16[1,336,6144]{2,1,0:T(8,128)(2,1)}, u32[]{:S(2)}) copy-start(bf16[1,336,6144]{2,1,0:T(8,128)(2,1)} %w_hbm.1) | copy-start | bytes 12386308

commit v2 on v1

v2 whole, which is shorter than its diff:
```python
import jax
import jax.numpy as jnp
from jax import lax
from jax.experimental import pallas as pl
from jax.experimental.pallas import tpu as pltpu
from jax.sharding import PartitionSpec as P

F32 = jnp.float32
BF16 = jnp.bfloat16
HALF = 768
META = 128
PART = HALF // 2
FIRST = META + PART
WIDE = HALF + META
SUB = 40
PAD = 48
CHUNK = 160
NT = (((1,), (1,)), ((), ()))


def kernel(cot, ids, probs, saved, w_hbm, dgate, dup, gw, ext, stage, tok_a, tok_b, ypack, rows, wv, before,
           hid, hid_t, coef_g, coef_u, g_sum, rs_out, rs_in, w_sem, x_sem, h_sem, a_sem, b_sem, y_sem, d_sem,
           r_sem):
    x, e, t = lax.axis_index("dp"), lax.axis_index("expert"), lax.axis_index("tensor")
    y, zhi = e // 4, e % 4
    zlo, c = t // 2, t % 2
    z = zhi * 8 + zlo
    width = saved.shape[3]

    def at(x_to, y_to, z_to, c_to):
        return (x_to, y_to * 4 + z_to // 8, (z_to % 8) * 2 + c_to)

    def send(src, dst, sems, index, to):
        copy = pltpu.make_async_remote_copy(
            src_ref=src, dst_ref=dst, send_sem=sems.at[(0,) + index], recv_sem=sems.at[(1,) + index],
            device_id=to, device_id_type=pl.DeviceIdType.MESH)
        copy.start()
        return copy

    load_w = pltpu.make_async_copy(
        w_hbm.at[0, :, pl.ds(pl.multiple_of(x * (2 * HALF), 128), 2 * HALF)], wv, w_sem)
    load_w.start()

    next_y, last_y, far_y = (y + 1) % 4, (y + 3) % 4, (y + 2) % 4
    sibling = at(x, y, z, 1 - c)
    partners = [at((x + dx) % 4, y, z, (c + dc) % 2) for dx in range(4) for dc in range(2) if dx or dc]
    partners += [at(x, y, (z + 8 * dz) % 32, c) for dz in (1, 2, 3)]
    partners += [at(x, y, (z + dz) % 32, c) for dz in (1, 31, 2, 30)]
    partners += [at(x, y_to, z, c) for y_to in (next_y, last_y, far_y)]
    barrier = pltpu.get_barrier_semaphore()
    for device in partners:
        pl.semaphore_signal(barrier, inc=1, device_id=device, device_id_type=pl.DeviceIdType.MESH)

    lane = lax.broadcasted_iota(jnp.int32, (2, META), 1)
    meta = jnp.zeros((2, META), F32)
    for k in range(4):
        meta = jnp.where(lane == k, ids[:, k:k + 1].astype(F32), meta)
        meta = jnp.where(lane == 4 + k, probs[:, k:k + 1].astype(F32), meta)
    for q in range(8):
        ext[q, :, META:WIDE] = cot[:, q * HALF:(q + 1) * HALF]
        ext[q, :, 0:META] = meta.astype(BF16)
    pl.semaphore_wait(barrier, len(partners))

    x_copies = []
    for dx in range(4):
        for dc in range(2):
            if dx or dc:
                xd, cd = (x + dx) % 4, (c + dc) % 2
                x_copies.append(send(ext.at[xd * 2 + cd], stage.at[x * 2 + c], x_sem, (dx * 2 + dc,),
                                     at(xd, y, z, cd)))
    stage[x * 2 + c] = ext[x * 2 + c]

    for copy in x_copies:
        copy.wait_recv()
    toks = (tok_a, tok_b)
    tok_a[zlo, zhi] = stage[:, :, 0:FIRST].reshape(16, FIRST)
    tok_b[zlo, zhi] = stage[:, :, FIRST:WIDE].reshape(16, PART)

    a_copies, b_copies = {}, {}
    for h in range(2):
        for k in (2, 1, 3):
            own = toks[h].at[zlo, zhi]
            a_copies[h, k] = send(own, own, a_sem, (h * 4 + k,), at(x, y, (z + 32 - 8 * k) % 32, c))

    def pass_on(h, way, k, held, far):
        origin = (z + 32 - way * held) % 32
        block = toks[h].at[origin % 8, (origin // 8 + k) % 4]
        index = h * 32 + (way + 1) // 2 * 16 + k * 4 + held + far - 1
        b_copies[h, way, k, held + far] = send(block, block, b_sem, (index,),
                                               at(x, y, (z + 32 + way * far) % 32, c))

    def spread(h, k):
        if k:
            a_copies[h, k].wait_recv()
        for way in (1, -1):
            pass_on(h, way, k, 0, 2)
            pass_on(h, way, k, 0, 1)

    def spread_on(h, k):
        for way in (1, -1):
            b_copies[h, way, k, 2].wait_recv()
            pass_on(h, way, k, 2, 1)
            if k in (0, 3 if way == 1 else 1):
                pass_on(h, way, k, 2, 2)

    def gathered(h):
        for way in (1, -1):
            for k in range(4):
                b_copies[h, way, k, 1].wait_recv()
                b_copies[h, way, k, 3].wait_recv()
            for k in (0, 3 if way == 1 else 1):
                b_copies[h, way, k, 4].wait_recv()

    for h in range(2):
        spread(h, 0)

    for part in range(4):
        both = saved[part].astype(F32)
        g, u = both[:, 0, :], both[:, 1, :]
        s = jax.nn.sigmoid(g)
        coef_g[part] = u * s * (1.0 + g * (1.0 - s))
        coef_u[part] = g * s
        hid[x, part, 0:SUB] = (g * s * u).astype(BF16)
        hid[x, part, SUB:PAD] = jnp.zeros((PAD - SUB, width), BF16)
    h_copies = [send(hid.at[x], hid.at[x], h_sem, (dx,), at((x + dx) % 4, y, z, c)) for dx in (1, 2, 3)]

    from_row = lax.broadcasted_iota(jnp.int32, (512, 512), 0)
    to_row = lax.broadcasted_iota(jnp.int32, (512, 512), 1)
    same = ((from_row >> 2) & 15) == ((to_row >> 2) & 15)
    before[...] = jnp.where(same & (from_row < to_row), 1.0, 0.0).astype(BF16)
    for h in range(2):
        for k in (1, 3, 2):
            spread(h, k)
    for h in range(2):
        for k in (0, 1, 3, 2):
            spread_on(h, k)
    gathered(0)

    meta = tok_a[:, :, :, 0:META].reshape(512, META)
    pick = (lax.broadcasted_iota(jnp.int32, (8, META), 0) ==
            lax.broadcasted_iota(jnp.int32, (8, META), 1)).astype(F32).astype(BF16)
    meta_t = lax.dot_general(pick, meta, NT, preferred_element_type=F32)
    step_y = lax.broadcasted_iota(jnp.int32, (8, 512), 0)
    expert = (((step_y + y) & 3) * 4 + zhi).astype(F32)
    named = jnp.zeros((8, 512), F32)
    prob = jnp.zeros((8, 512), F32)
    for k in range(4):
        hit = meta_t[k:k + 1, :] == expert
        named = named + jnp.where(hit, 1.0, 0.0)
        prob = prob + jnp.where(hit, meta_t[4 + k:5 + k, :], 0.0)
    place = jnp.dot(named.astype(BF16), before[...], preferred_element_type=F32)
    token = lax.broadcasted_iota(jnp.int32, (8, 512), 1)
    base = (((token >> 2) & 3) * SUB + ((token >> 4) & 3) * 10).astype(F32)
    slot = jnp.where(named > 0.5, base + place, -1.0)
    slots = lax.broadcasted_iota(jnp.int32, (CHUNK, 512), 0).astype(F32)

    y_copies, d_copies = {}, {}

    def pack(h):
        data = (tok_a[:, :, :, META:FIRST] if h == 0 else tok_b[...]).reshape(512, PART)
        for d in (2, 1, 3, 0):
            select = jnp.where(slots == slot[d:d + 1, :], prob[d:d + 1, :], 0.0).astype(BF16)
            packed = jnp.dot(select, data, preferred_element_type=F32).astype(BF16)
            own = rows.at[h, c, y]
            if d:
                ypack[h, d - 1] = packed
                y_copies[h, d] = send(ypack.at[h, d - 1], own, y_sem, (h * 4 + d,), at(x, (y + d) % 4, z, c))
            else:
                rows[h, c, y] = packed
                d_copies[h, 0] = send(own, own, d_sem, (h * 4,), sibling)

    pack(0)
    gathered(1)
    pack(1)

    for copy in h_copies:
        copy.wait_recv()
    load_w.wait()
    for part in range(4):
        chunk = jnp.concatenate([hid[r, part].astype(F32)[0:SUB] for r in range(4)], axis=0)
        hid_t[part * CHUNK:(part + 1) * CHUNK] = chunk.astype(BF16)

    chunks = (y, last_y, next_y, far_y)
    r_copies = []

    def share(h):
        for i, d in ((1, 1), (2, 3), (3, 2)):
            y_copies[h, d].wait_recv()
            block = rows.at[h, c, chunks[i]]
            d_copies[h, i] = send(block, block, d_sem, (h * 4 + i,), sibling)

    def product(h, i):
        d_copies[h, i].wait_recv()
        low = h * PART
        return (lax.dot_general(rows[h, 0, chunks[i]], wv[:, low:low + PART], NT, preferred_element_type=F32) +
                lax.dot_general(rows[h, 1, chunks[i]], wv[:, HALF + low:HALF + low + PART], NT,
                                preferred_element_type=F32))

    share(0)
    for i in range(4):
        g_sum[i] = product(0, i)
    share(1)
    for i, part in enumerate(chunks):
        gh = product(1, i) + g_sum[i]
        for r in range(4):
            rs_out[part, r, 0:SUB] = gh[r * SUB:(r + 1) * SUB].astype(BF16)
            rs_out[part, r, SUB:PAD] = jnp.zeros((PAD - SUB, width), BF16)
        r_copies.append([send(rs_out.at[part, (x + dx) % 4], rs_in.at[x, part], r_sem, (i, dx),
                              at((x + dx) % 4, y, z, c)) for dx in (1, 2, 3)])

    for core in range(2):
        for h in range(2):
            low = core * HALF + h * PART
            gw[:, low:low + PART] = lax.dot_general(
                hid_t[...], rows[h, core].reshape(4 * CHUNK, PART), (((0,), (0,)), ((), ())),
                preferred_element_type=F32).astype(BF16)

    for i, part in enumerate(chunks):
        for copy in r_copies[i]:
            copy.wait_recv()
        gh = rs_out[part, x].astype(F32)[0:SUB]
        for dx in (1, 2, 3):
            gh = gh + rs_in[(x + dx) % 4, part].astype(F32)[0:SUB]
        dgate[part] = (gh * coef_g[part]).astype(BF16)
        dup[part] = (gh * coef_u[part]).astype(BF16)

    sent = x_copies + h_copies
    for group in (a_copies, b_copies, y_copies, d_copies):
        sent += group.values()
    for group in r_copies:
        sent += group
    for copy in sent:
        copy.wait_send()


def per_device(grad_out, route_ids, route_probs, gate_up, w_down):
    width = gate_up.shape[5]
    vmem = pl.BlockSpec(memory_space=pltpu.VMEM)
    dma = pltpu.SemaphoreType.DMA
    dgate, dup, gw = pl.pallas_call(
        kernel,
        out_shape=(
            jax.ShapeDtypeStruct((4, SUB, width), BF16),
            jax.ShapeDtypeStruct((4, SUB, width), BF16),
            jax.ShapeDtypeStruct((width, 2 * HALF), BF16),
        ),
        in_specs=[vmem, vmem, vmem, vmem, pl.BlockSpec(memory_space=pl.ANY)],
        out_specs=(vmem, vmem, vmem),
        scratch_shapes=[
            pltpu.VMEM((8, 2, WIDE), BF16),
            pltpu.VMEM((8, 2, WIDE), BF16),
            pltpu.VMEM((8, 4, 16, FIRST), BF16),
            pltpu.VMEM((8, 4, 16, PART), BF16),
            pltpu.VMEM((2, 3, CHUNK, PART), BF16),
            pltpu.VMEM((2, 2, 4, CHUNK, PART), BF16),
            pltpu.VMEM((width, 2 * HALF), BF16),
            pltpu.VMEM((512, 512), BF16),
            pltpu.VMEM((4, 4, PAD, width), BF16),
            pltpu.VMEM((4 * CHUNK, width), BF16),
            pltpu.VMEM((4, SUB, width), F32),
            pltpu.VMEM((4, SUB, width), F32),
            pltpu.VMEM((4, CHUNK, width), F32),
            pltpu.VMEM((4, 4, PAD, width), BF16),
            pltpu.VMEM((4, 4, PAD, width), BF16),
            dma(()),
            dma((2, 8)),
            dma((2, 4)),
            dma((2, 8)),
            dma((2, 64)),
            dma((2, 8)),
            dma((2, 8)),
            dma((2, 4, 4)),
        ],
        compiler_params=pltpu.CompilerParams(
            collective_id=0, has_side_effects=True, vmem_limit_bytes=60 * 1024 * 1024
        ),
    )(grad_out, route_ids, route_probs, gate_up.reshape(4, SUB, 2, width), w_down)
    grad_pre = jnp.stack([dgate, dup], axis=2).reshape(gate_up.shape)
    return grad_pre, gw[None]


def solution(mesh):
    return jax.shard_map(
        per_device,
        mesh=mesh,
        in_specs=(
            P(("dp", "expert", "tensor"), None),
            P(("dp", "expert", "tensor"), None),
            P(("dp", "expert", "tensor"), None),
            P("dp", "expert", None, None, None, "tensor"),
            P("expert", "tensor", None),
        ),
        out_specs=(P("dp", "expert", None, None, None, "tensor"), P("expert", "tensor", "dp")),
        check_vma=False,
    )
```

time: 95.1 us -> 88.1 us (0.926)
  Pallas kernels: 86.1 us -> 82 us
  other arithmetic: 2.27 us -> 0.09 us
    pallas_call x1, Pallas kernels: 86.1 us -> 82 us  [per_device(): pl.pallas_call(kernel, out_shape=(jax.ShapeDtypeStruct((4, SUB, width), B...]
    another operation x2, local copies, waits for them, and re-layouts: 0.11 us -> 1.92 us  [per_device(): grad_pre = jnp.stack([dgate, dup], axis=2).reshape(gate_up.shape)]
    concatenate x2 -> x0, other arithmetic: 1.49 us -> none  [the longest x1 0.76 us: per_device(): jnp.concatenate([cot, jnp.broadcast_to(meta[None], (8, 2, META))], axis=2)]
    slice x1 -> x0, local copies, waits for them, and re-layouts: 1.49 us -> none  [per_device(): saved[:, :, 1]]
    unnamed x4 -> x2, local copies, waits for them, and re-layouts: 4.07 us -> 3.19 us
where the time goes in v2:
time: 88.1 us; the launch traced here: 87.9 us
  Pallas kernels  82 us (93%)
  local copies, waits for them, and re-layouts  5.11 us (6%)
    pallas_call x1, Pallas kernels, per_device(): pl.pallas_call(kernel, out_shape=(jax.ShapeDtypeStruct((4, SUB, width), B...  82 us
    unnamed x2, local copies, waits for them, and re-layouts  3.19 us
    another operation x2, local copies, waits for them, and re-layouts, per_device(): grad_pre = jnp.stack([dgate, dup], axis=2).reshape(gate_up.shape)  1.92 us

profile of v2, /device:TPU:1, one launch (start us, length us, event | category | flops | bytes accessed | tf_op | source)
XLA Modules:
  0.0 87.9 jit_solution(13890578225530936762)
XLA Ops:
  0.6 82.0 %shard_map.68 = (bf16[4,40,336]{2,1,0:T(8,128)(2,1)}, bf16[4,40,336]{2,1,0:T(8,128)(2,1)}, bf16[336,1536]{1,0:T(8,128)(2,1)}) custom-call(bf16[2,6144]{1,0:T(2,128)(2,1)} %cot.1, s32[2,4]{1,0:T(2,128)} %ids.1, bf16[2,4]{1,0:T(2,128)(2,1)} %probs.1, bf16[4,40,2,336]{3,2,1,0:T(2,128)(2,1)} %bitcast.3, bf16[1,336,6144]{2,1,0:T(8,128)(2,1)} %w_hbm.1), custom_call_target="tpu_custom_call" | custom-call | tf_op jit(solution)/shard_map/pallas_call | solution.py:240
  82.7 1.0 %stack.9 = bf16[1,1,16,10,1,336]{5,3,2,4,1,0:T(8,128)(2,1)S(1)} reshape(bf16[4,40,336]{2,1,0:T(8,128)(2,1)} %get-tuple-element.5) | data formatting | bytes 215040 | tf_op jit(solution)/shard_map/stack | solution.py:278
  83.6 1.0 %stack.10 = bf16[1,1,16,10,1,336]{5,3,2,4,1,0:T(8,128)(2,1)S(1)} reshape(bf16[4,40,336]{2,1,0:T(8,128)(2,1)} %get-tuple-element.6) | data formatting | bytes 215040 | tf_op jit(solution)/shard_map/stack | solution.py:278
  84.6 0.1 pad_maximum_fusion
  84.7 0.9 %copy.9 = bf16[1,1,16,10,2,336]{5,4,3,2,1,0:T(2,128)(2,1)} copy(bf16[1,1,16,10,2,336]{5,3,2,4,1,0:T(8,128)(2,1)S(1)} %pad_maximum_fusion) | data formatting | bytes 430080
  85.6 2.2 %copy.11 = bf16[1,336,1536]{2,1,0:T(8,128)(2,1)} copy(bf16[1,336,1536]{2,1,0:T(8,128)(2,1)} %bitcast.2) | data formatting | bytes 2064384

commit v3 on v2

--- a/solution.py
+++ b/solution.py
@@ -18,7 +18,7 @@
 NT = (((1,), (1,)), ((), ()))
 
 
-def kernel(cot, ids, probs, saved, w_hbm, dgate, dup, gw, ext, stage, tok_a, tok_b, ypack, rows, wv, before,
+def kernel(cot, ids, probs, saved, w_hbm, dpre, gw, ext, stage, tok_a, tok_b, ypack, rows, wv, before,
            hid, hid_t, coef_g, coef_u, g_sum, rs_out, rs_in, w_sem, x_sem, h_sem, a_sem, b_sem, y_sem, d_sem,
            r_sem):
     x, e, t = lax.axis_index("dp"), lax.axis_index("expert"), lax.axis_index("tensor")
@@ -221,8 +221,8 @@
         gh = rs_out[part, x].astype(F32)[0:SUB]
         for dx in (1, 2, 3):
             gh = gh + rs_in[(x + dx) % 4, part].astype(F32)[0:SUB]
-        dgate[part] = (gh * coef_g[part]).astype(BF16)
-        dup[part] = (gh * coef_u[part]).astype(BF16)
+        dpre[0, part] = (gh * coef_g[part]).astype(BF16)
+        dpre[1, part] = (gh * coef_u[part]).astype(BF16)
 
     sent = x_copies + h_copies
     for group in (a_copies, b_copies, y_copies, d_copies):
@@ -237,15 +237,14 @@
     width = gate_up.shape[5]
     vmem = pl.BlockSpec(memory_space=pltpu.VMEM)
     dma = pltpu.SemaphoreType.DMA
-    dgate, dup, gw = pl.pallas_call(
+    dpre, gw = pl.pallas_call(
         kernel,
         out_shape=(
-            jax.ShapeDtypeStruct((4, SUB, width), BF16),
-            jax.ShapeDtypeStruct((4, SUB, width), BF16),
+            jax.ShapeDtypeStruct((2, 4, SUB, width), BF16),
             jax.ShapeDtypeStruct((width, 2 * HALF), BF16),
         ),
         in_specs=[vmem, vmem, vmem, vmem, pl.BlockSpec(memory_space=pl.ANY)],
-        out_specs=(vmem, vmem, vmem),
+        out_specs=(vmem, vmem),
         scratch_shapes=[
             pltpu.VMEM((8, 2, WIDE), BF16),
             pltpu.VMEM((8, 2, WIDE), BF16),
@@ -275,7 +274,7 @@
             collective_id=0, has_side_effects=True, vmem_limit_bytes=60 * 1024 * 1024
         ),
     )(grad_out, route_ids, route_probs, gate_up.reshape(4, SUB, 2, width), w_down)
-    grad_pre = jnp.stack([dgate, dup], axis=2).reshape(gate_up.shape)
+    grad_pre = jnp.moveaxis(dpre, 0, 2).reshape(gate_up.shape)
     return grad_pre, gw[None]
 
 

time: 88.1 us -> 87 us (0.988)
  local copies, waits for them, and re-layouts: 5.11 us -> 4.07 us
    another operation x2 -> x0, local copies, waits for them, and re-layouts: 1.92 us -> none  [per_device(): grad_pre = jnp.stack([dgate, dup], axis=2).reshape(gate_up.shape)]
    transpose x0 -> x1, local copies, waits for them, and re-layouts: none -> 1.83 us  [per_device(): grad_pre = jnp.moveaxis(dpre, 0, 2).reshape(gate_up.shape)]
    unnamed x2 -> x1, local copies, waits for them, and re-layouts: 3.19 us -> 2.24 us
where the time goes in v3:
time: 87 us; the launch traced here: 86.7 us
  Pallas kernels  82 us (94%)
  local copies, waits for them, and re-layouts  4.07 us (5%)
    pallas_call x1, Pallas kernels, per_device(): pl.pallas_call(kernel, out_shape=(jax.ShapeDtypeStruct((2, 4, SUB, width)...  82 us
    unnamed x1, local copies, waits for them, and re-layouts  2.24 us
    transpose x1, local copies, waits for them, and re-layouts, per_device(): grad_pre = jnp.moveaxis(dpre, 0, 2).reshape(gate_up.shape)  1.83 us

profile of v3, /device:TPU:1, one launch (start us, length us, event | category | flops | bytes accessed | tf_op | source)
XLA Modules:
  0.0 86.7 jit_solution(14888848042924181281)
XLA Ops:
  0.6 82.0 %shard_map.68 = (bf16[2,4,40,336]{3,2,1,0:T(8,128)(2,1)}, bf16[336,1536]{1,0:T(8,128)(2,1)}) custom-call(bf16[2,6144]{1,0:T(2,128)(2,1)} %cot.1, s32[2,4]{1,0:T(2,128)} %ids.1, bf16[2,4]{1,0:T(2,128)(2,1)} %probs.1, bf16[4,40,2,336]{3,2,1,0:T(2,128)(2,1)} %bitcast.5, bf16[1,336,6144]{2,1,0:T(8,128)(2,1)} %w_hbm.1), custom_call_target="tpu_custom_call" | custom-call | tf_op jit(solution)/shard_map/pallas_call | solution.py:240
  82.7 1.8 %copy.8 = bf16[4,40,2,336]{3,2,1,0:T(2,128)(2,1)} copy(bf16[4,40,2,336]{3,1,0,2:T(8,128)(2,1)} %bitcast.7) | data formatting | bytes 430080 | tf_op jit(solution)/shard_map/transpose | solution.py:277
  84.5 2.2 %copy.10 = bf16[1,336,1536]{2,1,0:T(8,128)(2,1)} copy(bf16[1,336,1536]{2,1,0:T(8,128)(2,1)} %bitcast.4) | data formatting | bytes 2064384

commit v4 on v3

--- a/solution.py
+++ b/solution.py
@@ -199,8 +199,9 @@
     share(0)
     for i in range(4):
         g_sum[i] = product(0, i)
-    share(1)
     for i, part in enumerate(chunks):
+        if i == 1:
+            share(1)
         gh = product(1, i) + g_sum[i]
         for r in range(4):
             rs_out[part, r, 0:SUB] = gh[r * SUB:(r + 1) * SUB].astype(BF16)

time: 87 us -> 86.7 us (level)
  no operation moved by 1% of the time
where the time goes in v4:
time: 86.7 us; the launch traced here: 86.4 us
  Pallas kernels  81.7 us (94%)
  local copies, waits for them, and re-layouts  4.07 us (5%)
    pallas_call x1, Pallas kernels, per_device(): pl.pallas_call(kernel, out_shape=(jax.ShapeDtypeStruct((2, 4, SUB, width)...  81.7 us
    unnamed x1, local copies, waits for them, and re-layouts  2.24 us
    transpose x1, local copies, waits for them, and re-layouts, per_device(): grad_pre = jnp.moveaxis(dpre, 0, 2).reshape(gate_up.shape)  1.83 us

profile of v4, /device:TPU:1, one launch (start us, length us, event | category | flops | bytes accessed | tf_op | source)
XLA Modules:
  0.0 86.4 jit_solution(13120103242069482815)
XLA Ops:
  0.6 81.7 %shard_map.68 = (bf16[2,4,40,336]{3,2,1,0:T(8,128)(2,1)}, bf16[336,1536]{1,0:T(8,128)(2,1)}) custom-call(bf16[2,6144]{1,0:T(2,128)(2,1)} %cot.1, s32[2,4]{1,0:T(2,128)} %ids.1, bf16[2,4]{1,0:T(2,128)(2,1)} %probs.1, bf16[4,40,2,336]{3,2,1,0:T(2,128)(2,1)} %bitcast.5, bf16[1,336,6144]{2,1,0:T(8,128)(2,1)} %w_hbm.1), custom_call_target="tpu_custom_call" | custom-call | tf_op jit(solution)/shard_map/pallas_call | solution.py:241
  82.4 1.8 %copy.8 = bf16[4,40,2,336]{3,2,1,0:T(2,128)(2,1)} copy(bf16[4,40,2,336]{3,1,0,2:T(8,128)(2,1)} %bitcast.7) | data formatting | bytes 430080 | tf_op jit(solution)/shard_map/transpose | solution.py:278
  84.2 2.2 %copy.10 = bf16[1,336,1536]{2,1,0:T(8,128)(2,1)} copy(bf16[1,336,1536]{2,1,0:T(8,128)(2,1)} %bitcast.4) | data formatting | bytes 2064384
